TPU v7x, 128 devices: a whole 4x4x4 slice. The times are simulated.
128 devices in a mesh: blk: 8 (over x_lo, z), grp: 16 (over y, x_hi, core).
Axes of the slice: x: 4 (x_hi: 2, x_lo: 2; x = x_hi * 2 + x_lo), y: 4, z: 4, core: 2. Of those that a mesh axis runs over, the one named last changes fastest.
Arguments:
- global_desc: bfloat16 [65536, 1024], P(('grp', 'blk')), may hold values from -0.1875 to 0.1875
- key_points: bfloat16 [512, 512, 256], P(('grp', 'blk')), may hold values from -1 to 1
- pair_first: int32 [1536], P(('grp', 'blk')), may hold values from 0 to 3
- pair_second: int32 [1536], P(('grp', 'blk')), may hold values from 0 to 63, as said below
Outputs:
- expanded: bfloat16 [65536, 1024], P(('grp', 'blk'))
- confidence: float32 [1536, 2, 512], P(('grp', 'blk'))
Inputs may be any that keep to these rules, and one draw needn't show every extreme that they name: pair_second[p] = g * 4 + r names image r of the device at grp index g and the owner's blk index. Among one device's 12 pairs at most 2 name images of one source device, and every device has a source with exactly 2.
All inputs are finite; a program needn't handle non-finite values.
Results may differ from a plain program's by a relative error of at most 0.0029.
Values may be sent and summed in bfloat16 or wider, within the bound.
No kernel may reach another device: no remote copies, remote signals or barrier semaphores. Data moves between devices by JAX's collectives and lax.ppermute only.
A program may use at most 128 MiB of HBM per device.

v0:
```python
import math

import jax
import jax.numpy as jnp
from jax import lax
from jax.sharding import PartitionSpec as P

softmax_sharpness = 10.0
epsilon = 1e-06


def dual_confidence(similarity_scores):
    row_sum_exponent = jax.nn.logsumexp(similarity_scores, axis=2)
    col_total = jax.nn.logsumexp(similarity_scores, axis=1)
    match_log_probability = (
        2.0 * similarity_scores
        - row_sum_exponent[:, :, None]
        - col_total[:, None, :]
        + 2.0 * math.log(similarity_scores.shape[2])
    )
    return jnp.stack(
        [jnp.max(match_log_probability, axis=2), jnp.max(match_log_probability, axis=1)], axis=1
    )


def on_device(global_desc, key_points, pair_first, pair_second):
    piece = lax.all_gather(global_desc, "blk", axis=0, tiled=True)
    sims = lax.dot_general(
        global_desc, piece, (((1,), (1,)), ((), ())), preferred_element_type=jnp.float32
    )
    weights = jnp.maximum(sims, 0.0).astype(jnp.bfloat16)
    totals = jnp.dot(weights, piece, preferred_element_type=jnp.float32)
    scale = lax.rsqrt(jnp.mean(totals * totals, axis=1, keepdims=True) + epsilon)
    expanded = (totals * scale).astype(jnp.bfloat16)
    pair_count = pair_second.shape[0]
    empty = jnp.zeros((pair_count, key_points.shape[1], key_points.shape[2]), jnp.bfloat16)
    piece = lax.all_gather(key_points, "grp", axis=0, tiled=True)
    inside = (pair_second >= 0) & (pair_second < piece.shape[0])
    rows = piece[jnp.clip(pair_second, 0, piece.shape[0] - 1)]
    fetched = jnp.where(inside[:, None, None], rows, empty)
    image_local_keypoints = key_points[pair_first]
    similarity_scores = (
        jnp.einsum(
            "pad,pbd->pab", image_local_keypoints, fetched, preferred_element_type=jnp.float32
        )
        * softmax_sharpness
    )
    confidence = dual_confidence(similarity_scores)
    return (expanded, confidence)


def solution(mesh):
    in_specs = (
        P(("grp", "blk"), None),
        P(("grp", "blk"), None, None),
        P(("grp", "blk")),
        P(("grp", "blk")),
    )
    out_specs = (P(("grp", "blk"), None), P(("grp", "blk"), None, None))
    return jax.shard_map(
        on_device, mesh=mesh, in_specs=in_specs, out_specs=out_specs, check_vma=False
    )
```

profile of v0, /device:TPU:1, one launch (start us, length us, event | category | flops | bytes accessed | tf_op | source)
XLA Modules:
  0.0 246.3 jit_solution(10006412042853610813)
XLA Ops:
  7.2 0.0 copy-start
  7.2 0.0 all-gather.3.cloned.1.call-start
  7.2 0.7 all-gather.3.cloned.1.call-update
  7.9 0.0 all-gather.5.cloned.1.call-start
  8.0 0.7 all-gather.5.cloned.1.call-update
  8.7 0.7 compare_select_fusion.1
  9.3 2.0 gather_fusion
  11.3 0.0 copy-done
  11.4 93.7 %all-gather.3.cloned.1.call-done = bf16[4096,1024]{1,0:T(8,128)(2,1)} async-done(((bf16[512,1024]{1,0:T(8,128)(2,1)}), bf16[4096,1024]{1,0:T(8,128)(2,1)}) %all-gather.3.cloned.1.call-update) | async-done | bytes 8388624 | tf_op jit(solution)/shard_map/all_gather | solution.py:27
  105.0 16.3 %multiply_reduce_fusion.2 = (f32[512]{0:T(512)S(1)}, f32[512,1024]{1,0:T(8,128)}) fusion(bf16[4096,1024]{1,0:T(8,128)(2,1)} %all-gather.3.cloned.1.call-done, bf16[512,1024]{1,0:T(8,128)(2,1)} %param.4), kind=kOutput, calls=%fused_computation.14 | convolution fusion | flops 8595177472 | bytes 11536384 | tf_op jit(solution)/shard_map/dot_general | solution.py:32
  121.3 2.7 %multiply_convert_fusion = bf16[512,1024]{1,0:T(8,128)(2,1)} fusion(f32[512,1024]{1,0:T(8,128)} %get-tuple-element.11, f32[512]{0:T(512)S(1)} %add_rsqrt_fusion), kind=kLoop, calls=%fused_computation.13 | loop fusion | flops 1048576 | bytes 3147776 | tf_op jit(solution)/shard_map/convert_element_type | solution.py:34
  124.1 91.6 %all-gather.5.cloned.1.call-done = bf16[64,512,256]{2,1,0:T(8,128)(2,1)} async-done(((bf16[4,512,256]{2,1,0:T(8,128)(2,1)}), bf16[64,512,256]{2,1,0:T(8,128)(2,1)}) %all-gather.5.cloned.1.call-update) | async-done | bytes 16777232 | tf_op jit(solution)/shard_map/all_gather | solution.py:37
  215.7 8.3 %gather_fusion.1 = bf16[12,512,256]{2,1,0:T(8,128)(2,1)} fusion(bf16[64,512,256]{2,1,0:T(8,128)(2,1)} %all-gather.5.cloned.1.call-done, s32[1024]{0:T(1024)S(1)} %pad_clamp_fusion), kind=kCustom, calls=%fused_computation.1 | custom fusion | bytes 6291504 | tf_op jit(solution)/shard_map/gather | solution.py:39
  224.0 3.9 %multiply_reduce_fusion.1 = (f32[12,512]{1,0:T(8,128)S(1)}, f32[12,512,512]{2,1,0:T(8,128)S(1)}) fusion(bf16[12,512,256]{2,1,0:T(8,128)(2,1)S(1)} %gather_fusion, bf16[12,512,256]{2,1,0:T(8,128)(2,1)} %gather_fusion.1, pred[12]{0:T(512)(128)(4,1)S(1)} %compare_and_fusion), kind=kOutput, calls=%fused_computation.6 | convolution fusion | flops 1618470912 | bytes 18898956 | tf_op jit(solution)/shard_map/pad,pbd->pab/dot_general | solution.py:43
  227.9 5.3 %exponential_reduce_fusion.1 = (f32[12,512]{1,0:T(8,128)S(1)}, f32[12,512]{1,0:T(8,128)S(1)}) fusion(f32[12,512,512]{2,1,0:T(8,128)S(1)} %get-tuple-element.13, f32[12,512]{1,0:T(8,128)S(1)} %is-finite_select_fusion.1), kind=kLoop, calls=%fused_computation.4 | loop fusion | flops 12570624 | bytes 12656640 | tf_op jit(solution)/shard_map/reduce_sum | solution.py:13
  233.2 2.1 exponential_reduce_fusion
  235.3 3.5 %fusion.1 = (f32[12,512]{1,0:T(8,128)S(1)}, f32[12,512]{1,0:T(8,128)S(1)}) fusion(f32[12,512,512]{2,1,0:T(8,128)S(1)} %get-tuple-element.13, f32[12,512]{1,0:T(8,128)S(1)} %log_add_fusion, f32[12,512]{1,0:T(8,128)S(1)} %get-tuple-element.15), kind=kLoop, calls=%fused_computation.8 | loop fusion | flops 18862080 | bytes 12681216 | tf_op jit(solution)/shard_map/reduce_max | solution.py:22
  238.8 0.7 copy.7
  (9 shorter events, 0.1 us)
Async XLA Ops:
  7.2 4.1 %copy-start = (s32[12]{0:T(128)S(1)}, s32[12]{0:T(128)}, u32[]{:S(2)}) copy-start(s32[12]{0:T(128)} %param.7) | copy-start | bytes 148
  7.2 97.8 %all-gather.3.cloned.1.call-start = ((), (), s32[]{:S(2)}) async-start(), calls=%async_computation | async-start | bytes 9437184 | tf_op jit(solution)/shard_map/all_gather | solution.py:27
  7.9 207.8 %all-gather.5.cloned.1.call-start = ((), (), s32[]{:S(2)}) async-start(), calls=%async_computation.1 | async-start | bytes 17825792 | tf_op jit(solution)/shard_map/all_gather | solution.py:37
Sparse Core Ops, SparseCore 0:
  9.7 95.3 all-gather.2
  107.5 108.1 all-gather.4
where the time goes:
time: 247 us; the launch traced here: 246 us
  waiting for transfers between devices  187 us (76%)
  matrix products  20.2 us (8%)
  other arithmetic  14.3 us (6%)
  between operations  14.1 us (6%)
  local copies, waits for them, and re-layouts  10.9 us (4%)
    all_gather x1, waiting for transfers between devices, on_device(): piece = lax.all_gather(global_desc, 'blk', axis=0, tiled=True)  93.7 us
    all_gather x1, waiting for transfers between devices, on_device(): piece = lax.all_gather(key_points, 'grp', axis=0, tiled=True)  91.6 us
    dot_general x1, matrix products, on_device(): totals = jnp.dot(weights, piece, preferred_element_type=jnp.float32)  16.3 us
    gather x1, local copies, waits for them, and re-layouts, on_device(): rows = piece[jnp.clip(pair_second, 0, piece.shape[0] - 1)]  8.28 us
    reduce_sum x1, other arithmetic, dual_confidence(): row_sum_exponent = jax.nn.logsumexp(similarity_scores, axis=2)  5.27 us
  transfers between devices with their start and end apart: 2, of which 2 were waited for; matrix products, arithmetic and copies ran while one was open for 9% of the time, Pallas kernels for 0%

commit v1 on v0

v1 whole, which is shorter than its diff:
```python
import functools
import math

import jax
import jax.numpy as jnp
from jax import lax
from jax.experimental import pallas as pl
from jax.experimental.pallas import tpu as pltpu
from jax.sharding import PartitionSpec as P

softmax_sharpness = 10.0
epsilon = 1e-06
log2_e = 1.4426950408889634
vmem_bytes = 12 * 2**20

def steps(axis, turn):
    pairs = []
    for device in range(128):
        blk, grp = device // 16, device % 16
        hop = turn if grp % 2 == 0 else -turn
        if axis == "z":
            blk = blk // 4 * 4 + (blk + hop) % 4
        else:
            grp = (grp // 4 + hop) % 4 * 4 + grp % 4
        pairs.append((device, blk * 16 + grp))
    return pairs


BOTH = ("blk", "grp")
Z_1, Z_2, Y_1, Y_2 = steps("z", 1), steps("z", -1), steps("y", 1), steps("y", -1)
X_PAIR = [(i, i ^ 4) for i in range(8)]
CORE = [(i, i ^ 1) for i in range(16)]
X_FAR = [(i, i ^ 2) for i in range(16)]
X_FAR_CORE = [(i, i ^ 3) for i in range(16)]


def fold_lanes(op, x):
    return op(op(x[:, 0:128], x[:, 128:256]), op(x[:, 256:384], x[:, 384:512]))


def confidences(t, row_lse, col_lse, out_ref, where):
    rows, m = t[0].shape
    half = 0.5 / softmax_sharpness
    offset = 2.0 * math.log(m)
    row_half, col_half = row_lse * half, col_lse * half
    best = jnp.full((8, m), -jnp.inf, jnp.float32)
    row_best = []
    for k, part in enumerate(t):
        part = part[...]
        sl = slice(k * rows, (k + 1) * rows)
        tile = jnp.transpose(jnp.broadcast_to(row_half[:, sl], (128, rows)))
        tile = jnp.concatenate([tile] * (m // 128), axis=1)
        best = jnp.maximum(best, jnp.max((part - tile).reshape(rows // 8, 8, m), axis=0))
        row_best.append(
            jnp.max(jnp.transpose(fold_lanes(jnp.maximum, part - col_half)), axis=0, keepdims=True)
        )
    out_ref[where, 0:1, :] = jnp.concatenate(row_best, axis=1) * (1.0 / half) - row_lse + offset
    out_ref[where, 1:2, :] = jnp.max(best, axis=0, keepdims=True) * (1.0 / half) - col_lse + offset


def match_two(pairs, out_ref):
    rows = 256
    sums = []
    for a_ref, b_ref, t_ref, _ in pairs:
        n, m = t_ref.shape
        col = jnp.zeros((8, m), jnp.float32)
        row_sums = []
        for k in range(n // rows):
            sl = slice(k * rows, (k + 1) * rows)
            t = lax.dot_general(
                a_ref[sl, :], b_ref[...], (((1,), (1,)), ((), ())), preferred_element_type=jnp.float32
            )
            t_ref[sl, :] = t
            e = jnp.exp2(t * (softmax_sharpness * log2_e))
            row_sums.append(jnp.sum(jnp.transpose(fold_lanes(jnp.add, e)), axis=0, keepdims=True))
            col = col + jnp.sum(e.reshape(rows // 8, 8, m), axis=0)
        sums.append((jnp.concatenate(row_sums, axis=1), jnp.sum(col, axis=0, keepdims=True)))
    low = functools.reduce(jnp.minimum, [x for both in sums for x in both])
    high = functools.reduce(jnp.maximum, [x for both in sums for x in both])
    in_range = (jnp.min(low) > 1e-25) & (jnp.max(high) < 1e30)
    for (_, _, t_ref, where), (row_sum, col_sum) in zip(pairs, sums):
        parts = [t_ref.at[k:k + rows, :] for k in range(0, t_ref.shape[0], rows)]
        confidences(parts, jnp.log(row_sum), jnp.log(col_sum), out_ref, where)

    @pl.when(jnp.logical_not(in_range))
    def _():
        for _, _, t_ref, where in pairs:
            n = t_ref.shape[0]
            s = t_ref[...] * softmax_sharpness
            peak = jnp.max(s, axis=0, keepdims=True)
            col_lse = jnp.log(jnp.sum(jnp.exp(s - peak), axis=0, keepdims=True)) + peak
            peak = jnp.max(s, axis=1, keepdims=True)
            row_lse = jnp.log(jnp.sum(jnp.exp(s - peak), axis=1, keepdims=True)) + peak
            row_lse = jnp.transpose(jnp.broadcast_to(row_lse, (n, 128)))[0:1, :]
            parts = [t_ref.at[k:k + rows, :] for k in range(0, n, rows)]
            confidences(parts, row_lse, col_lse, out_ref, where)


def pairs_kernel(place_ref, meta_ref, *rest, owners, steps, skip):
    rest = list(rest)
    firsts = [rest.pop(0) for _ in range(owners)]
    seconds = {step: rest.pop(0) for step in steps}
    before_ref = rest.pop(0) if skip else None
    out_ref, list_ref, a_0, b_0, t_0, a_1, b_1, t_1 = rest
    lists, _, count = meta_ref.shape
    n = t_0.shape[0]
    mine, my_y = place_ref[0], place_ref[1]
    turn = 1 + 2 * place_ref[2]
    if skip:
        out_ref[...] = before_ref[...]

    total = jnp.int32(0)
    for owner in range(lists):
        for p in range(count):
            second = meta_ref[owner, 1, p]
            source = lax.shift_right_logical(second, 2)
            step = ((lax.shift_right_logical(source, 2) - my_y + 4) * turn) & 3
            hit = (source & 3) == mine
            if skip:
                done_owners, done_steps = skip
                if owner < done_owners:
                    hit = hit & functools.reduce(
                        jnp.logical_and, [step != k for k in done_steps]
                    )
            elif len(steps) < 4:
                hit = hit & functools.reduce(jnp.logical_or, [step == k for k in steps])
            list_ref[total] = (
                (owner + (owner * count + p) * 256) + meta_ref[owner, 0, p] * 4 + step * 16 + (second & 3) * 64
            )
            total = total + hit.astype(jnp.int32)

    def load(i, a_ref, b_ref):
        code = list_ref[jnp.minimum(i, total - 1)]
        owner = code & 3
        image = lax.shift_right_logical(code, 2) & 3
        step = lax.shift_right_logical(code, 4) & 3
        row = lax.shift_right_logical(code, 6) & 3
        rows = pl.ds(pl.multiple_of(image * n, n), n)
        for k, ref in enumerate(firsts[:3]):
            @pl.when(owner == k)
            def _():
                a_ref[...] = ref[image] if len(ref.shape) == 3 else ref[rows, :]
        for k, ref in enumerate(firsts[3:]):
            @pl.when((owner == 3) & (image == k))
            def _():
                a_ref[...] = ref[...]
        for k, ref in seconds.items():
            @pl.when(step == k)
            def _():
                b_ref[...] = ref[row]
        return lax.shift_right_logical(code, 8)

    def two(i, carry):
        where_0 = load(2 * i, a_0, b_0)
        where_1 = load(2 * i + 1, a_1, b_1)
        match_two(((a_0, b_0, t_0, where_0), (a_1, b_1, t_1, where_1)), out_ref)
        return carry

    lax.fori_loop(0, lax.shift_right_logical(total + 1, 1), two, 0)


def match_pairs(place, meta, firsts, seconds, before=None, skip=None):
    _, n, width = seconds[0].shape
    count = meta.shape[2]
    smem = pl.BlockSpec(memory_space=pltpu.SMEM)
    vmem = pl.BlockSpec(memory_space=pltpu.VMEM)
    arrays = (*firsts, *seconds.values()) + (() if before is None else (before,))
    return pl.pallas_call(
        functools.partial(pairs_kernel, owners=len(firsts), steps=tuple(seconds), skip=skip),
        out_shape=jax.ShapeDtypeStruct((4 * count, 2, n), jnp.float32),
        in_specs=[smem, smem] + [vmem] * len(arrays),
        out_specs=vmem,
        scratch_shapes=[
            pltpu.SMEM((4 * count + 1,), jnp.int32),
        ] + 2 * [
            pltpu.VMEM((n, width), jnp.bfloat16),
            pltpu.VMEM((n, width), jnp.bfloat16),
            pltpu.VMEM((n, n), jnp.float32),
        ],
        compiler_params=pltpu.CompilerParams(vmem_limit_bytes=vmem_bytes),
        cost_estimate=pl.CostEstimate(
            flops=n, bytes_accessed=n, transcendentals=0
        ),
        name="match_pairs",
    )(place, meta, *arrays)


def after(x, *deps):
    return lax.optimization_barrier((x,) + deps)[0]


def block_kernel(own_ref, *rest, pieces, first, last):
    rest = list(rest)
    blocks = [rest.pop(0) for _ in range(pieces)]
    total_ref = None if first else rest.pop(0)
    out_ref, weights_ref = rest[:2]
    wide = 256
    n = own_ref.shape[1]
    at = 0
    for block in blocks:
        for q in range(0, block.shape[0], wide):
            sims = lax.dot_general(
                own_ref[...], block[q:q + wide, :], (((1,), (1,)), ((), ())),
                preferred_element_type=jnp.float32,
            )
            weights_ref[:, at:at + wide] = jnp.maximum(sims, 0.0).astype(jnp.bfloat16)
            at += wide
    square = None
    for c in range(0, n, wide):
        total = None if first else total_ref[:, c:c + wide]
        at = 0
        for block in blocks:
            h = block.shape[0]
            part = jnp.dot(
                weights_ref[:, at:at + h], block[:, c:c + wide], preferred_element_type=jnp.float32
            )
            total = part if total is None else total + part
            at += h
        if last:
            total_ref[:, c:c + wide] = total
            folded = total[:, :128] * total[:, :128] + total[:, 128:] * total[:, 128:]
            square = folded if square is None else square + folded
        else:
            out_ref[:, c:c + wide] = total
    if last:
        scale = lax.rsqrt(jnp.sum(square, axis=1, keepdims=True) * (1.0 / n) + epsilon)
        for c in range(0, n, wide):
            out_ref[:, c:c + wide] = (total_ref[:, c:c + wide] * scale).astype(out_ref.dtype)


def add_blocks(own, blocks, total=None, last=False):
    rows, n = own.shape
    count = sum(b.shape[0] for b in blocks)
    vmem = pl.BlockSpec(memory_space=pltpu.VMEM)
    args = (own, *blocks) + (() if total is None else (total,))
    return pl.pallas_call(
        functools.partial(block_kernel, pieces=len(blocks), first=total is None, last=last),
        out_shape=jax.ShapeDtypeStruct((rows, n), jnp.bfloat16 if last else jnp.float32),
        in_specs=[vmem] * len(args),
        out_specs=vmem,
        scratch_shapes=[pltpu.VMEM((rows, count), jnp.bfloat16)],
        compiler_params=pltpu.CompilerParams(vmem_limit_bytes=vmem_bytes),
        cost_estimate=pl.CostEstimate(
            flops=n, bytes_accessed=n, transcendentals=0
        ),
        name="add_blocks",
    )(*args)


def join_kernel(a_ref, b_ref, out_ref):
    out_ref[: a_ref.shape[0], :] = a_ref[...]
    out_ref[a_ref.shape[0]:, :] = b_ref[...]


def join(a, b):
    vmem = pl.BlockSpec(memory_space=pltpu.VMEM)
    return pl.pallas_call(
        join_kernel,
        out_shape=jax.ShapeDtypeStruct((a.shape[0] + b.shape[0], a.shape[1]), a.dtype),
        in_specs=[vmem] * 2,
        out_specs=vmem,
        compiler_params=pltpu.CompilerParams(vmem_limit_bytes=vmem_bytes),
        cost_estimate=pl.CostEstimate(flops=1, bytes_accessed=1, transcendentals=0),
        name="join",
    )(a, b)


def split_kernel(a_ref, *rest):
    outs, sems = rest[:-1], rest[-1]
    rows = outs[0].shape[0]
    copies = [
        pltpu.make_async_copy(a_ref.at[i * rows:(i + 1) * rows], out, sems.at[i])
        for i, out in enumerate(outs)
    ]
    for copy in copies:
        copy.start()
    for copy in copies:
        copy.wait()


def split(a, count):
    hbm = pl.BlockSpec(memory_space=pl.ANY)
    rows, width = a.shape[0] // count // 16 * 16, a.shape[1]
    return pl.pallas_call(
        split_kernel,
        out_shape=[jax.ShapeDtypeStruct((rows, width), a.dtype)] * count,
        in_specs=[hbm],
        out_specs=[hbm] * count,
        scratch_shapes=[pltpu.SemaphoreType.DMA((count,))],
        compiler_params=pltpu.CompilerParams(vmem_limit_bytes=vmem_bytes),
        cost_estimate=pl.CostEstimate(flops=1, bytes_accessed=1, transcendentals=0),
        name="split",
    )(a)


def on_device(global_desc, key_points, pair_first, pair_second):
    g = lax.axis_index("grp")
    images, n, width = key_points.shape
    count = pair_second.shape[0]

    def move(v, perm):
        return lax.ppermute(v, BOTH, perm)

    own = global_desc
    own_1 = move(own, Z_1)
    own_2 = move(own, Z_2)
    pair = lax.ppermute(own, "blk", X_PAIR)
    k_core = lax.ppermute(key_points, "grp", CORE)
    k_1 = move(key_points, Y_1)
    lists = jnp.stack([pair_first, pair_second])
    near = jnp.stack([lists, lax.ppermute(lists, "grp", CORE)])
    rows = near.reshape(4, count).astype(jnp.bfloat16)
    rows = jnp.zeros((16, width), jnp.bfloat16).at[:4, :count].set(rows)
    sheet = jnp.concatenate([key_points.reshape(images * n, width), rows])
    own_1, own_2, pair, sheet, near = lax.optimization_barrier((own_1, own_2, pair, sheet, near))

    pair_1 = move(pair, Z_1)
    own_3_pair_2 = move(join(own_2, pair), Z_2)
    k_3 = move(after(k_1, pair), Y_1)
    k_2 = move(after(key_points, pair, k_core), Y_2)
    sheet_far = lax.ppermute(sheet, "grp", X_FAR)
    total = add_blocks(own, (own, own_1, own_2, pair))
    place = jnp.stack([g % 4, g // 4, g % 2])
    found = match_pairs(place, after(near, total), (key_points, k_core), {0: key_points, 1: k_2, 3: k_1})


    pair_3 = move(after(pair_1, found, k_3), Z_1)
    total = add_blocks(own, (pair_1,), total)
    far_core = [lax.ppermute(v, "grp", CORE) for v in split(after(sheet_far, found, total), images)]
    far = sheet_far[images * n:images * n + 4, :count].astype(jnp.int32).reshape(2, 2, count)
    every = jnp.concatenate([near, far])
    found = match_pairs(
        place, every, (key_points, k_core, sheet_far, *far_core),
        {0: key_points, 1: k_2, 2: k_3, 3: k_1}, found, (2, (0, 1, 3)),
    )
    found = found.reshape(4, count, 2, n)
    back = [
        found[0],
        lax.ppermute(found[1], "grp", CORE),
        lax.ppermute(found[2], "grp", X_FAR),
        lax.ppermute(found[3], "grp", X_FAR_CORE),
    ]
    total = add_blocks(own, (own_3_pair_2,), after(total, found))
    expanded = add_blocks(own, (pair_3,), total, last=True)
    handler = (pair_second // 4) % 4 ^ (g % 4)
    handler = after(handler, expanded)[:, None, None]
    confidence = jnp.where(
        handler == 0, back[0], jnp.where(handler == 1, back[1], jnp.where(handler == 2, back[2], back[3]))
    )
    return (expanded, confidence)


def solution(mesh):
    in_specs = (
        P(("grp", "blk"), None),
        P(("grp", "blk"), None, None),
        P(("grp", "blk")),
        P(("grp", "blk")),
    )
    out_specs = (P(("grp", "blk"), None), P(("grp", "blk"), None, None))
    return jax.shard_map(
        on_device, mesh=mesh, in_specs=in_specs, out_specs=out_specs, check_vma=False
    )
```

time: 247 us -> 103 us (0.42)
  waiting for transfers between devices: 187 us -> 24.4 us
  Pallas kernels: 0 us -> 44.5 us
  starting transfers between devices: 0.08 us -> 23.5 us
  matrix products: 20.2 us -> 0 us
  between operations: 14.1 us -> 0.83 us
  other arithmetic: 14.3 us -> 3.86 us
  local copies, waits for them, and re-layouts: 10.9 us -> 5.44 us
    all_gather x2 -> x0, waiting for transfers between devices: 185 us -> none  [the longest x1 93.7 us: on_device(): piece = lax.all_gather(global_desc, 'blk', axis=0, tiled=True)]
    pallas_call x0 -> x8, Pallas kernels: none -> 44.5 us  [the longest x2 26.9 us: match_pairs(): pl.pallas_call(functools.partial(pairs_kernel, owners=len(firsts), steps=...]
    ppermute x0 -> x19, waiting for transfers between devices: none -> 24.4 us  [the longest x8 20.7 us: move(): return lax.ppermute(v, BOTH, perm)]
    ppermute x0 -> x19, starting transfers between devices: none -> 23.5 us  [the longest x8 13.5 us: move(): return lax.ppermute(v, BOTH, perm)]
    dot_general x2 -> x0, matrix products: 20.2 us -> none  [the longest x1 16.3 us: on_device(): totals = jnp.dot(weights, piece, preferred_element_type=jnp.float32)]
    gather x2 -> x0, local copies, waits for them, and re-layouts: 10.3 us -> none  [the longest x1 8.28 us: on_device(): rows = piece[jnp.clip(pair_second, 0, piece.shape[0] - 1)]]
    reduce_sum x2 -> x0, other arithmetic: 7.36 us -> none  [the longest x1 5.27 us: dual_confidence(): row_sum_exponent = jax.nn.logsumexp(similarity_scores, axis=2)]
    unnamed x3 -> x18, local copies, waits for them, and re-layouts: 0.66 us -> 5.42 us
  transfers between devices with their start and end apart: 2 -> 19, of which waited for: 2 -> 8; matrix products, arithmetic and copies ran while one was open for 9% -> 3% of each run, Pallas kernels for 0% -> 43%
where the time goes in v1:
time: 103 us
  Pallas kernels  44.5 us (43%)
  waiting for transfers between devices  24.4 us (24%)
  starting transfers between devices  23.5 us (23%)
  local copies, waits for them, and re-layouts  5.44 us (5%)
  other arithmetic  3.86 us (4%)
    pallas_call x2, Pallas kernels, match_pairs(): pl.pallas_call(functools.partial(pairs_kernel, owners=len(firsts), steps=...  26.9 us
    ppermute x8, waiting for transfers between devices, move(): return lax.ppermute(v, BOTH, perm)  20.7 us
    pallas_call x4, Pallas kernels, add_blocks(): pl.pallas_call(functools.partial(block_kernel, pieces=len(blocks), first=...  14.7 us
    ppermute x8, starting transfers between devices, move(): return lax.ppermute(v, BOTH, perm)  13.5 us
    unnamed x18, local copies, waits for them, and re-layouts  5.42 us
    ppermute x1, starting transfers between devices, on_device(): lax.ppermute(found[3], 'grp', X_FAR_CORE)  3.54 us
    ppermute x1, starting transfers between devices, on_device(): sheet_far = lax.ppermute(sheet, 'grp', X_FAR)  2.74 us
    pallas_call x1, Pallas kernels, join(): pl.pallas_call(join_kernel, out_shape=jax.ShapeDtypeStruct((a.shape[0] +...  2.72 us
  transfers between devices with their start and end apart: 19, of which 8 were waited for; matrix products, arithmetic and copies ran while one was open for 3% of the time, Pallas kernels for 43%

profile of v1, /device:TPU:1, one launch (start us, length us, event | category | flops | bytes accessed | tf_op | source)
XLA Modules:
  0.0 102.5 jit_solution(11965893882849582092)
XLA Ops:
  0.6 0.0 copy-start.1
  0.6 4.7 %collective-permute-start = (bf16[512,1024]{1,0:T(8,128)(2,1)}, bf16[512,1024]{1,0:T(8,128)(2,1)S(1)}, u32[]{:S(2)}, u32[]{:S(2)}) collective-permute-start(bf16[512,1024]{1,0:T(8,128)(2,1)} %own_ref.7), channel_id=1, source_target_pairs={{0,16},{1,49},{2,18},{3,51},{4,20},{5,53},{6,22},{7,55},{8,24},{9,... | collective-permute-start | bytes 3145736 | tf_op jit(solution)/shard_map/ppermute | solution.py:302
  5.3 0.0 collective-permute-start.1
  5.3 1.2 %collective-permute-start.2 = (bf16[512,1024]{1,0:T(8,128)(2,1)}, bf16[512,1024]{1,0:T(8,128)(2,1)}, u32[]{:S(2)}, u32[]{:S(2)}) collective-permute-start(bf16[512,1024]{1,0:T(8,128)(2,1)} %own_ref.7), channel_id=1, source_target_pairs={{0,64},{16,80},{32,96},{48,112},{64,0},{80,16},{96,32},{112,48},{1... | collective-permute-start | bytes 3145736 | tf_op jit(solution)/shard_map/ppermute | solution.py:307
  6.5 1.3 %collective-permute-start.5 = (bf16[4,512,256]{2,1,0:T(8,128)(2,1)}, bf16[4,512,256]{2,1,0:T(8,128)(2,1)S(1)}, u32[]{:S(2)}, u32[]{:S(2)}) collective-permute-start(bf16[4,512,256]{2,1,0:T(8,128)(2,1)} %rest_7_.1), channel_id=1, source_target_pairs={{0,1},{1,0},{2,3},{3,2},{4,5},{5,4},{6,7},{7,6},{8,9},{9,8},{10,11... | collective-permute-start | bytes 3145736 | tf_op jit(solution)/shard_map/ppermute | solution.py:308
  7.8 0.7 fusion.4
  8.5 0.0 collective-permute-start.3
  8.5 1.6 %collective-permute-done.3 = s32[2,12]{1,0:T(2,128)S(1)} collective-permute-done((s32[2,12]{1,0:T(2,128)S(1)}, s32[2,12]{1,0:T(2,128)S(1)}, u32[]{:S(2)}, u32[]{:S(2)}) %collective-permute-start.3) | collective-permute-done | bytes 128 | tf_op jit(solution)/shard_map/ppermute | solution.py:311
  10.1 2.7 %collective-permute-start.7 = (bf16[4,512,256]{2,1,0:T(8,128)(2,1)}, bf16[4,512,256]{2,1,0:T(8,128)(2,1)}, u32[]{:S(2)}, u32[]{:S(2)}) collective-permute-start(bf16[4,512,256]{2,1,0:T(8,128)(2,1)} %rest_7_.1), channel_id=1, source_target_pairs={{0,4},{1,13},{2,6},{3,15},{4,8},{5,1},{6,10},{7,3},{8,12},{9,5},{1... | collective-permute-start | bytes 3145736 | tf_op jit(solution)/shard_map/ppermute | solution.py:302
  12.9 2.3 %fusion.1 = bf16[2064,256]{1,0:T(8,128)(2,1)} fusion(bf16[4,12]{1,0:T(4,128)(2,1)S(1)} %bitcast.13, bf16[2048,256]{1,0:T(8,128)(2,1)} %bitcast.12), kind=kLoop, calls=%fused_computation.2 | loop fusion | flops 3170304 | bytes 2105440 | tf_op jit(solution)/shard_map/concatenate | solution.py:314
  15.2 12.1 %collective-permute-done.rest_1_ = bf16[512,1024]{1,0:T(8,128)(2,1)S(1)} collective-permute-done((bf16[512,1024]{1,0:T(8,128)(2,1)}, bf16[512,1024]{1,0:T(8,128)(2,1)S(1)}, u32[]{:S(2)}, u32[]{:S(2)}) %collective-permute-start) | collective-permute-done | bytes 1048608 | tf_op jit(solution)/shard_map/ppermute | solution.py:302
  27.3 0.0 copy-start.6
  27.3 1.0 copy-done.6
  28.3 1.5 %collective-permute-done.1.rest_2_.a_ref = bf16[512,1024]{1,0:T(8,128)(2,1)S(1)} collective-permute-done((bf16[512,1024]{1,0:T(8,128)(2,1)}, bf16[512,1024]{1,0:T(8,128)(2,1)S(1)}, u32[]{:S(2)}, u32[]{:S(2)}) %collective-permute-start.1) | collective-permute-done | bytes 1048608 | tf_op jit(solution)/shard_map/ppermute | solution.py:302
  29.8 0.0 collective-permute-done.2.rest_3_.b_ref
  29.8 0.0 copy-start
  29.8 3.3 %collective-permute-start.4 = (bf16[512,1024]{1,0:T(8,128)(2,1)}, bf16[512,1024]{1,0:T(8,128)(2,1)}, u32[]{:S(2)}, u32[]{:S(2)}) collective-permute-start(bf16[512,1024]{1,0:T(8,128)(2,1)} %collective-permute-done.2.rest_3_.b_ref), channel_id=1, source_target_pairs={{0,16},{1,49},{2,18},{3,51},{4,20},{5,53},{6,22},{7,55},{8,24},{9,... | collective-permute-start | bytes 3145736 | tf_op jit(solution)/shard_map/ppermute | solution.py:302
  33.1 0.0 collective-permute-done.5.rest_1_
  33.1 0.0 copy-start.2
  33.1 1.0 copy-done.2
  34.0 0.0 copy-done.1
  34.0 1.3 %collective-permute-start.6 = (bf16[4,512,256]{2,1,0:T(8,128)(2,1)S(1)}, bf16[4,512,256]{2,1,0:T(8,128)(2,1)}, u32[]{:S(2)}, u32[]{:S(2)}) collective-permute-start(bf16[4,512,256]{2,1,0:T(8,128)(2,1)S(1)} %copy-done.1), channel_id=1, source_target_pairs={{0,12},{1,5},{2,14},{3,7},{4,0},{5,9},{6,2},{7,11},{8,4},{9,13},{1... | collective-permute-start | bytes 3145736 | tf_op jit(solution)/shard_map/ppermute | solution.py:302
  35.3 0.0 collective-permute-done.7.rest_4_.rest_10_
  35.3 1.5 %collective-permute-start.8 = (bf16[4,512,256]{2,1,0:T(8,128)(2,1)}, bf16[4,512,256]{2,1,0:T(8,128)(2,1)}, u32[]{:S(2)}, u32[]{:S(2)}) collective-permute-start(bf16[4,512,256]{2,1,0:T(8,128)(2,1)} %collective-permute-done.7.rest_4_.rest_10_), channel_id=1, source_target_pairs={{0,4},{1,13},{2,6},{3,15},{4,8},{5,1},{6,10},{7,3},{8,12},{9,5},{1... | collective-permute-start | bytes 3145736 | tf_op jit(solution)/shard_map/ppermute | solution.py:302
  36.9 2.7 %join.1 = bf16[1024,1024]{1,0:T(8,128)(2,1)} custom-call(bf16[512,1024]{1,0:T(8,128)(2,1)S(1)} %collective-permute-done.1.rest_2_.a_ref, bf16[512,1024]{1,0:T(8,128)(2,1)} %collective-permute-done.2.rest_3_.b_ref), custom_call_target="tpu_custom_call" | custom-call | flops 1 | bytes 1 | tf_op jit(solution)/shard_map/join/pallas_call | solution.py:257
  39.6 1.0 copy-done.4
  40.6 0.0 collective-permute-start.10
  40.6 2.7 %collective-permute-start.11 = (bf16[2064,256]{1,0:T(8,128)(2,1)}, bf16[2064,256]{1,0:T(8,128)(2,1)S(1)}, u32[]{:S(2)}, u32[]{:S(2)}) collective-permute-start(bf16[2064,256]{1,0:T(8,128)(2,1)} %fusion.1), channel_id=1, source_target_pairs={{0,2},{1,3},{2,0},{3,1},{4,6},{5,7},{6,4},{7,5},{8,10},{9,11},{10,... | collective-permute-start | bytes 3170312 | tf_op jit(solution)/shard_map/ppermute | solution.py:321
  43.3 0.1 pad_add_fusion.3.place_ref
  43.4 0.0 copy-done
  43.4 1.2 %copy-done.5 = bf16[512,1024]{1,0:T(8,128)(2,1)S(1)} copy-done((bf16[512,1024]{1,0:T(8,128)(2,1)S(1)}, bf16[512,1024]{1,0:T(8,128)(2,1)}, u32[]{:S(2)}) %copy-start.5) | copy-done | bytes 1048600
  44.6 1.2 %copy-done.7 = bf16[512,1024]{1,0:T(8,128)(2,1)S(1)} copy-done((bf16[512,1024]{1,0:T(8,128)(2,1)S(1)}, bf16[512,1024]{1,0:T(8,128)(2,1)}, u32[]{:S(2)}) %copy-start.7) | copy-done | bytes 1048600
  45.9 5.8 %add_blocks.4.rest_1_ = f32[512,1024]{1,0:T(8,128)S(1)} custom-call(bf16[512,1024]{1,0:T(8,128)(2,1)S(1)} %copy-done, bf16[512,1024]{1,0:T(8,128)(2,1)S(1)} %copy-done, bf16[512,1024]{1,0:T(8,128)(2,1)S(1)} %copy-done.7, bf16[512,1024]{1,0:T(8,128)(2,1)S(1)} %copy-done.5, bf16[512,1024]{1,0:T(8,128)(2,1)} %collective-permute-done.2.rest_3_.b_ref), custom_call_target="tpu_custom_call" | custom-call | flops 1024 | bytes 1024 | tf_op jit(solution)/shard_map/add_blocks/pallas_call | solution.py:236
  51.7 7.1 %collective-permute-done.6.rest_3_.rest_8_ = bf16[4,512,256]{2,1,0:T(8,128)(2,1)} collective-permute-done((bf16[4,512,256]{2,1,0:T(8,128)(2,1)S(1)}, bf16[4,512,256]{2,1,0:T(8,128)(2,1)}, u32[]{:S(2)}, u32[]{:S(2)}) %collective-permute-start.6) | collective-permute-done | bytes 1048608 | tf_op jit(solution)/shard_map/ppermute | solution.py:302
  58.8 0.0 copy-done.3
  58.8 13.0 %match_pairs.2.rest_11_ = f32[48,2,512]{2,1,0:T(2,128)S(1)} custom-call(s32[3]{0:T(128)S(1)} %pad_add_fusion.3.place_ref, s32[2,2,12]{2,1,0:T(2,128)S(1)} %get-tuple-element.33.meta_ref, bf16[4,512,256]{2,1,0:T(8,128)(2,1)S(1)} %copy-done.1, bf16[4,512,256]{2,1,0:T(8,128)(2,1)S(1)} %copy-done.3, bf16[4,512,256]{2,1,0:T(8,128)(2,1)S(1)} %copy-done.1, ...), custom_call_target="tpu_custom_call" | custom-call | flops 512 | bytes 512 | tf_op jit(solution)/shard_map/match_pairs/pallas_call | solution.py:168
  71.8 0.0 copy-start.8
  71.8 0.0 collective-permute-done.4.rest_0_
  71.8 0.0 collective-permute-done.8.rest_9_
  71.8 0.1 collective-permute-start.9
  71.9 2.5 %add_blocks.5.rest_1_ = f32[512,1024]{1,0:T(8,128)S(1)} custom-call(bf16[512,1024]{1,0:T(8,128)(2,1)S(1)} %copy-done, bf16[512,1024]{1,0:T(8,128)(2,1)} %collective-permute-done.4.rest_0_, f32[512,1024]{1,0:T(8,128)S(1)} %add_blocks.4.rest_1_), custom_call_target="tpu_custom_call" | custom-call | flops 1024 | bytes 1024 | tf_op jit(solution)/shard_map/add_blocks/pallas_call | solution.py:236
  74.5 0.0 collective-permute-done.11.a_ref.rest_2_
  74.5 0.1 split.1
  74.6 0.1 collective-permute-start.12
  74.7 0.5 collective-permute-start.13
  75.2 0.3 collective-permute-start.14
  75.5 0.8 collective-permute-done.12.rest_3_
  76.2 0.1 collective-permute-start.15
  76.4 0.0 copy-done.8
  76.4 0.2 collective-permute-done.13.rest_4_
  76.6 0.4 collective-permute-done.14.rest_5_
  77.0 0.8 collective-permute-done.15.rest_6_
  77.8 13.9 %match_pairs.3 = f32[48,2,512]{2,1,0:T(2,128)S(1)} custom-call(s32[3]{0:T(128)S(1)} %pad_add_fusion.3.place_ref, s32[4,2,12]{2,1,0:T(2,128)S(1)} %pad_add_fusion.meta_ref, bf16[4,512,256]{2,1,0:T(8,128)(2,1)S(1)} %copy-done.1, bf16[4,512,256]{2,1,0:T(8,128)(2,1)S(1)} %copy-done.3, bf16[2064,256]{1,0:T(8,128)(2,1)S(1)} %collective-permute-done.11.a_ref.rest_2_, ...), custom_call_target="tpu_custom_call" | custom-call | flops 512 | bytes 512 | tf_op jit(solution)/shard_map/match_pairs/pallas_call | solution.py:168
  91.6 0.1 collective-permute-start.16
  91.7 0.1 collective-permute-start.17
  91.8 3.5 %collective-permute-start.18 = (f32[12,2,512]{2,1,0:T(2,128)S(1)}, f32[12,2,512]{2,1,0:T(2,128)S(1)}, u32[]{:S(2)}, u32[]{:S(2)}) collective-permute-start(f32[12,2,512]{2,1,0:T(2,128)S(1)} %get-tuple-element.44), channel_id=1, source_target_pairs={{0,3},{1,2},{2,1},{3,0},{4,7},{5,6},{6,5},{7,4},{8,11},{9,10},{10,... | collective-permute-start | bytes 147464 | tf_op jit(solution)/shard_map/ppermute | solution.py:341
  95.4 0.0 collective-permute-done.10.rest_0_
  95.4 4.0 %add_blocks.6.rest_1_ = f32[512,1024]{1,0:T(8,128)S(1)} custom-call(bf16[512,1024]{1,0:T(8,128)(2,1)S(1)} %copy-done, bf16[1024,1024]{1,0:T(8,128)(2,1)} %collective-permute-done.10.rest_0_, f32[512,1024]{1,0:T(8,128)S(1)} %add_blocks.5.rest_1_), custom_call_target="tpu_custom_call" | custom-call | flops 1024 | bytes 1024 | tf_op jit(solution)/shard_map/add_blocks/pallas_call | solution.py:236
  99.3 0.0 collective-permute-done.9.rest_0_
  99.3 2.4 %add_blocks.7 = bf16[512,1024]{1,0:T(8,128)(2,1)} custom-call(bf16[512,1024]{1,0:T(8,128)(2,1)S(1)} %copy-done, bf16[512,1024]{1,0:T(8,128)(2,1)S(1)} %collective-permute-done.9.rest_0_, f32[512,1024]{1,0:T(8,128)S(1)} %add_blocks.6.rest_1_), custom_call_target="tpu_custom_call" | custom-call | flops 1024 | bytes 1024 | tf_op jit(solution)/shard_map/add_blocks/pallas_call | solution.py:236
  101.8 0.0 collective-permute-done.16
  101.8 0.0 collective-permute-done.17
  101.8 0.0 collective-permute-done.18
  101.8 0.7 slice_select_fusion
  (11 shorter events, 0.1 us)
Async XLA Ops:
  0.6 33.4 %copy-start.1 = (bf16[4,512,256]{2,1,0:T(8,128)(2,1)S(1)}, bf16[4,512,256]{2,1,0:T(8,128)(2,1)}, u32[]{:S(2)}) copy-start(bf16[4,512,256]{2,1,0:T(8,128)(2,1)} %rest_7_.1) | copy-start | bytes 3145732
  0.6 26.7 %collective-permute-start = (bf16[512,1024]{1,0:T(8,128)(2,1)}, bf16[512,1024]{1,0:T(8,128)(2,1)S(1)}, u32[]{:S(2)}, u32[]{:S(2)}) collective-permute-start(bf16[512,1024]{1,0:T(8,128)(2,1)} %own_ref.7), channel_id=1, source_target_pairs={{0,16},{1,49},{2,18},{3,51},{4,20},{5,53},{6,22},{7,55},{8,24},{9,... | collective-permute-start | bytes 3145736 | tf_op jit(solution)/shard_map/ppermute | solution.py:302
  5.3 24.5 %collective-permute-start.1 = (bf16[512,1024]{1,0:T(8,128)(2,1)}, bf16[512,1024]{1,0:T(8,128)(2,1)S(1)}, u32[]{:S(2)}, u32[]{:S(2)}) collective-permute-start(bf16[512,1024]{1,0:T(8,128)(2,1)} %own_ref.7), channel_id=1, source_target_pairs={{0,48},{1,17},{2,50},{3,19},{4,52},{5,21},{6,54},{7,23},{8,56},{9,... | collective-permute-start | bytes 3145736 | tf_op jit(solution)/shard_map/ppermute | solution.py:302
  5.3 24.5 %collective-permute-start.2 = (bf16[512,1024]{1,0:T(8,128)(2,1)}, bf16[512,1024]{1,0:T(8,128)(2,1)}, u32[]{:S(2)}, u32[]{:S(2)}) collective-permute-start(bf16[512,1024]{1,0:T(8,128)(2,1)} %own_ref.7), channel_id=1, source_target_pairs={{0,64},{16,80},{32,96},{48,112},{64,0},{80,16},{96,32},{112,48},{1... | collective-permute-start | bytes 3145736 | tf_op jit(solution)/shard_map/ppermute | solution.py:307
  6.5 26.6 %collective-permute-start.5 = (bf16[4,512,256]{2,1,0:T(8,128)(2,1)}, bf16[4,512,256]{2,1,0:T(8,128)(2,1)S(1)}, u32[]{:S(2)}, u32[]{:S(2)}) collective-permute-start(bf16[4,512,256]{2,1,0:T(8,128)(2,1)} %rest_7_.1), channel_id=1, source_target_pairs={{0,1},{1,0},{2,3},{3,2},{4,5},{5,4},{6,7},{7,6},{8,9},{9,8},{10,11... | collective-permute-start | bytes 3145736 | tf_op jit(solution)/shard_map/ppermute | solution.py:308
  8.5 1.6 %collective-permute-start.3 = (s32[2,12]{1,0:T(2,128)S(1)}, s32[2,12]{1,0:T(2,128)S(1)}, u32[]{:S(2)}, u32[]{:S(2)}) collective-permute-start(s32[2,12]{1,0:T(2,128)S(1)} %get-tuple-element.50), channel_id=1, source_target_pairs={{0,1},{1,0},{2,3},{3,2},{4,5},{5,4},{6,7},{7,6},{8,9},{9,8},{10,11... | collective-permute-start | bytes 296 | tf_op jit(solution)/shard_map/ppermute | solution.py:311
  10.1 25.2 %collective-permute-start.7 = (bf16[4,512,256]{2,1,0:T(8,128)(2,1)}, bf16[4,512,256]{2,1,0:T(8,128)(2,1)}, u32[]{:S(2)}, u32[]{:S(2)}) collective-permute-start(bf16[4,512,256]{2,1,0:T(8,128)(2,1)} %rest_7_.1), channel_id=1, source_target_pairs={{0,4},{1,13},{2,6},{3,15},{4,8},{5,1},{6,10},{7,3},{8,12},{9,5},{1... | collective-permute-start | bytes 3145736 | tf_op jit(solution)/shard_map/ppermute | solution.py:302
  27.3 1.0 copy-start.6
  29.8 13.6 %copy-start = (bf16[512,1024]{1,0:T(8,128)(2,1)S(1)}, bf16[512,1024]{1,0:T(8,128)(2,1)}, u32[]{:S(2)}) copy-start(bf16[512,1024]{1,0:T(8,128)(2,1)} %own_ref.7) | copy-start | bytes 3145732
  29.8 42.0 %collective-permute-start.4 = (bf16[512,1024]{1,0:T(8,128)(2,1)}, bf16[512,1024]{1,0:T(8,128)(2,1)}, u32[]{:S(2)}, u32[]{:S(2)}) collective-permute-start(bf16[512,1024]{1,0:T(8,128)(2,1)} %collective-permute-done.2.rest_3_.b_ref), channel_id=1, source_target_pairs={{0,16},{1,49},{2,18},{3,51},{4,20},{5,53},{6,22},{7,55},{8,24},{9,... | collective-permute-start | bytes 3145736 | tf_op jit(solution)/shard_map/ppermute | solution.py:302
  33.1 1.0 copy-start.2
  34.0 24.7 %collective-permute-start.6 = (bf16[4,512,256]{2,1,0:T(8,128)(2,1)S(1)}, bf16[4,512,256]{2,1,0:T(8,128)(2,1)}, u32[]{:S(2)}, u32[]{:S(2)}) collective-permute-start(bf16[4,512,256]{2,1,0:T(8,128)(2,1)S(1)} %copy-done.1), channel_id=1, source_target_pairs={{0,12},{1,5},{2,14},{3,7},{4,0},{5,9},{6,2},{7,11},{8,4},{9,13},{1... | collective-permute-start | bytes 3145736 | tf_op jit(solution)/shard_map/ppermute | solution.py:302
  35.3 36.5 %collective-permute-start.8 = (bf16[4,512,256]{2,1,0:T(8,128)(2,1)}, bf16[4,512,256]{2,1,0:T(8,128)(2,1)}, u32[]{:S(2)}, u32[]{:S(2)}) collective-permute-start(bf16[4,512,256]{2,1,0:T(8,128)(2,1)} %collective-permute-done.7.rest_4_.rest_10_), channel_id=1, source_target_pairs={{0,4},{1,13},{2,6},{3,15},{4,8},{5,1},{6,10},{7,3},{8,12},{9,5},{1... | collective-permute-start | bytes 3145736 | tf_op jit(solution)/shard_map/ppermute | solution.py:302
  39.6 1.0 copy-start.4
  40.6 54.8 %collective-permute-start.10 = (bf16[1024,1024]{1,0:T(8,128)(2,1)}, bf16[1024,1024]{1,0:T(8,128)(2,1)}, u32[]{:S(2)}, u32[]{:S(2)}) collective-permute-start(bf16[1024,1024]{1,0:T(8,128)(2,1)} %join.1), channel_id=1, source_target_pairs={{0,48},{1,17},{2,50},{3,19},{4,52},{5,21},{6,54},{7,23},{8,56},{9,... | collective-permute-start | bytes 6291464 | tf_op jit(solution)/shard_map/ppermute | solution.py:302
  40.6 33.9 %collective-permute-start.11 = (bf16[2064,256]{1,0:T(8,128)(2,1)}, bf16[2064,256]{1,0:T(8,128)(2,1)S(1)}, u32[]{:S(2)}, u32[]{:S(2)}) collective-permute-start(bf16[2064,256]{1,0:T(8,128)(2,1)} %fusion.1), channel_id=1, source_target_pairs={{0,2},{1,3},{2,0},{3,1},{4,6},{5,7},{6,4},{7,5},{8,10},{9,11},{10,... | collective-permute-start | bytes 3170312 | tf_op jit(solution)/shard_map/ppermute | solution.py:321
  43.4 1.2 %copy-start.5 = (bf16[512,1024]{1,0:T(8,128)(2,1)S(1)}, bf16[512,1024]{1,0:T(8,128)(2,1)}, u32[]{:S(2)}) copy-start(bf16[512,1024]{1,0:T(8,128)(2,1)} %copy-done.4) | copy-start | bytes 3145732
  44.6 1.2 %copy-start.7 = (bf16[512,1024]{1,0:T(8,128)(2,1)S(1)}, bf16[512,1024]{1,0:T(8,128)(2,1)}, u32[]{:S(2)}) copy-start(bf16[512,1024]{1,0:T(8,128)(2,1)} %copy-done.6) | copy-start | bytes 3145732
  45.9 12.9 %copy-start.3 = (bf16[4,512,256]{2,1,0:T(8,128)(2,1)S(1)}, bf16[4,512,256]{2,1,0:T(8,128)(2,1)}, u32[]{:S(2)}) copy-start(bf16[4,512,256]{2,1,0:T(8,128)(2,1)} %copy-done.2) | copy-start | bytes 3145732
  71.8 4.6 %copy-start.8 = (s32[12]{0:T(128)S(1)}, s32[12]{0:T(128)}, u32[]{:S(2)}) copy-start(s32[12]{0:T(128)} %param.9) | copy-start | bytes 148
  71.8 27.5 %collective-permute-start.9 = (bf16[512,1024]{1,0:T(8,128)(2,1)}, bf16[512,1024]{1,0:T(8,128)(2,1)S(1)}, u32[]{:S(2)}, u32[]{:S(2)}) collective-permute-start(bf16[512,1024]{1,0:T(8,128)(2,1)} %collective-permute-done.4.rest_0_), channel_id=1, source_target_pairs={{0,16},{1,49},{2,18},{3,51},{4,20},{5,53},{6,22},{7,55},{8,24},{9,... | collective-permute-start | bytes 3145736 | tf_op jit(solution)/shard_map/ppermute | solution.py:302
  74.6 1.6 %collective-permute-start.12 = (bf16[512,256]{1,0:T(8,128)(2,1)S(1)}, bf16[512,256]{1,0:T(8,128)(2,1)S(1)}, u32[]{:S(2)}, u32[]{:S(2)}) collective-permute-start(bf16[512,256]{1,0:T(8,128)(2,1)S(1)} %get-tuple-element.40), channel_id=1, source_target_pairs={{0,1},{1,0},{2,3},{3,2},{4,5},{5,4},{6,7},{7,6},{8,9},{9,8},{10,11... | collective-permute-start | bytes 786440 | tf_op jit(solution)/shard_map/ppermute | solution.py:329
  74.7 1.9 %collective-permute-start.13 = (bf16[512,256]{1,0:T(8,128)(2,1)S(1)}, bf16[512,256]{1,0:T(8,128)(2,1)S(1)}, u32[]{:S(2)}, u32[]{:S(2)}) collective-permute-start(bf16[512,256]{1,0:T(8,128)(2,1)S(1)} %get-tuple-element.41), channel_id=1, source_target_pairs={{0,1},{1,0},{2,3},{3,2},{4,5},{5,4},{6,7},{7,6},{8,9},{9,8},{10,11... | collective-permute-start | bytes 786440 | tf_op jit(solution)/shard_map/ppermute | solution.py:329
  75.2 1.8 %collective-permute-start.14 = (bf16[512,256]{1,0:T(8,128)(2,1)S(1)}, bf16[512,256]{1,0:T(8,128)(2,1)S(1)}, u32[]{:S(2)}, u32[]{:S(2)}) collective-permute-start(bf16[512,256]{1,0:T(8,128)(2,1)S(1)} %get-tuple-element.42), channel_id=1, source_target_pairs={{0,1},{1,0},{2,3},{3,2},{4,5},{5,4},{6,7},{7,6},{8,9},{9,8},{10,11... | collective-permute-start | bytes 786440 | tf_op jit(solution)/shard_map/ppermute | solution.py:329
  76.2 1.5 %collective-permute-start.15 = (bf16[512,256]{1,0:T(8,128)(2,1)S(1)}, bf16[512,256]{1,0:T(8,128)(2,1)S(1)}, u32[]{:S(2)}, u32[]{:S(2)}) collective-permute-start(bf16[512,256]{1,0:T(8,128)(2,1)S(1)} %get-tuple-element.43), channel_id=1, source_target_pairs={{0,1},{1,0},{2,3},{3,2},{4,5},{5,4},{6,7},{7,6},{8,9},{9,8},{10,11... | collective-permute-start | bytes 786440 | tf_op jit(solution)/shard_map/ppermute | solution.py:329
  91.6 10.1 %collective-permute-start.16 = (f32[12,2,512]{2,1,0:T(2,128)S(1)}, f32[12,2,512]{2,1,0:T(2,128)S(1)}, u32[]{:S(2)}, u32[]{:S(2)}) collective-permute-start(f32[12,2,512]{2,1,0:T(2,128)S(1)} %get-tuple-element.46), channel_id=1, source_target_pairs={{0,1},{1,0},{2,3},{3,2},{4,5},{5,4},{6,7},{7,6},{8,9},{9,8},{10,11... | collective-permute-start | bytes 147464 | tf_op jit(solution)/shard_map/ppermute | solution.py:339
  91.7 10.0 %collective-permute-start.17 = (f32[12,2,512]{2,1,0:T(2,128)S(1)}, f32[12,2,512]{2,1,0:T(2,128)S(1)}, u32[]{:S(2)}, u32[]{:S(2)}) collective-permute-start(f32[12,2,512]{2,1,0:T(2,128)S(1)} %get-tuple-element.45), channel_id=1, source_target_pairs={{0,2},{1,3},{2,0},{3,1},{4,6},{5,7},{6,4},{7,5},{8,10},{9,11},{10,... | collective-permute-start | bytes 147464 | tf_op jit(solution)/shard_map/ppermute | solution.py:340
  91.8 9.9 %collective-permute-start.18 = (f32[12,2,512]{2,1,0:T(2,128)S(1)}, f32[12,2,512]{2,1,0:T(2,128)S(1)}, u32[]{:S(2)}, u32[]{:S(2)}) collective-permute-start(f32[12,2,512]{2,1,0:T(2,128)S(1)} %get-tuple-element.44), channel_id=1, source_target_pairs={{0,3},{1,2},{2,1},{3,0},{4,7},{5,6},{6,5},{7,4},{8,11},{9,10},{10,... | collective-permute-start | bytes 147464 | tf_op jit(solution)/shard_map/ppermute | solution.py:341
